TPU v7x, 32 devices: a whole 2x2x4 slice. The times are simulated.
32 devices in a mesh: groups: 2 (over y), cuts: 2 (over x), row: 4 (over z), sub: 2 (over core).
Axes of the slice: x: 2, y: 2, z: 4, core: 2. Of those that a mesh axis runs over, the one named last changes fastest.
Arguments:
- hop: bfloat16 [48, 6, 128, 128], P(('groups', 'row')), parts along dimension 0, may hold values from -0.21875 to 0.21875
- pattern: int32 [48, 6], P(('groups', 'row')), parts along dimension 0, may hold values from 0 to 23, as said below
- vectors: bfloat16 [2, 6144, 512], P('cuts', ('groups', 'row'), 'sub'), parts along dimension 1, may hold values from -6 to 6
- counts: int32 [4], P(('groups', 'cuts')), parts along dimension 0, may hold values from 256 to 512, as said below
- center: float32 [4], P(('groups', 'cuts')), parts along dimension 0, may hold values from -1 to 1
- halfwidth: float32 [4], P(('groups', 'cuts')), parts along dimension 0, may hold values from 1.5 to 3
Outputs:
- margin: float32 [4, 2, 256, 512], P(('groups', 'cuts'), 'sub', 'row'), parts along dimension 0
There are 2 independent parts, one for each index of `groups`. A program takes and returns all parts, laid end to end along the dimension named above; each array names one. Nothing has to cross between parts.
Inputs may be any that keep to these rules, and one draw needn't show every extreme that they name: `pattern`: block row i's stored blocks lie in block columns (i + o) mod 24 for 6 distinct offsets o between -3 and 3; the offsets 0, -3 and 3 appear in every block row. `counts`: at least one slice has all 512 vectors live.
All inputs are finite; a program needn't handle non-finite values.
Results may differ from a plain program's by a relative error of at most 0.00061.
Values may be sent and summed in bfloat16 or wider, within the bound.
A program may use at most 64 MiB of HBM per device.

v0:
```python
import jax
import jax.numpy as jnp
from jax import lax
from jax.sharding import PartitionSpec as P

W = 3


def with_halo(block, sides, width):
    for axis, dim in sides:
        count = lax.axis_size(axis)
        forward = [(i, i + 1) for i in range(count - 1)]
        forward.append((count - 1, 0))
        backward = [(target, source) for source, target in forward]
        low = lax.ppermute(
            lax.slice_in_dim(block, block.shape[dim] - width, None, axis=dim), axis, forward
        )
        high = lax.ppermute(lax.slice_in_dim(block, 0, width, axis=dim), axis, backward)
        block = jnp.concatenate([low, block, high], axis=dim)
    return block


def body(hop, pattern, vectors, counts, center, halfwidth):
    rows_dev = hop.shape[0]
    block = hop.shape[2]
    half = vectors.shape[2]
    row_count = lax.axis_size("row")
    total_blocks = rows_dev * row_count
    order_total = total_blocks * block
    first_block = lax.axis_index("row") * rows_dev
    local_index = (pattern - first_block + W) % total_blocks
    column_ids = lax.axis_index("sub") * half + jnp.arange(half, dtype=jnp.int32)
    live = (column_ids < counts[0]).astype(jnp.bfloat16)
    start = vectors[0] * live[None, :]
    shift_value = center[0]
    width_value = halfwidth[0]

    def apply_hop(field):
        extended = with_halo(field, (("row", 0),), W * block)
        blocks = extended.reshape(rows_dev + 2 * W, block, half)
        total = jnp.zeros((rows_dev, block, half), jnp.float32)
        for k in range(pattern.shape[1]):
            picked = jnp.take(blocks, local_index[:, k], axis=0)
            total = total + jnp.einsum(
                "rij,rjn->rin", hop[:, k], picked, preferred_element_type=jnp.float32
            )
        return total.reshape(rows_dev * block, half)

    first_image = apply_hop(start)
    step_one = ((first_image - shift_value * start.astype(jnp.float32)) / width_value).astype(
        jnp.bfloat16
    )
    second_image = apply_hop(step_one)
    filtered = (
        2.0 * (second_image - shift_value * step_one.astype(jnp.float32)) / width_value
        - start.astype(jnp.float32)
    ).astype(jnp.bfloat16)
    share = half // row_count
    full_cols = lax.all_gather(filtered, "sub", axis=1, tiled=True)
    term = jnp.einsum("rn,rm->nm", filtered, full_cols, preferred_element_type=jnp.float32)
    gram = lax.psum_scatter(term, "row", scatter_dimension=0, tiled=True)
    margin = gram / order_total
    return margin.reshape(1, 1, share, margin.shape[1])


def solution(mesh):
    in_specs = (
        P(("groups", "row"), None, None, None),
        P(("groups", "row"), None),
        P("cuts", ("groups", "row"), "sub"),
        P(("groups", "cuts")),
        P(("groups", "cuts")),
        P(("groups", "cuts")),
    )
    out_specs = P(("groups", "cuts"), "sub", "row", None)
    return jax.shard_map(body, mesh=mesh, in_specs=in_specs, out_specs=out_specs, check_vma=False)
```

profile of v0, /device:TPU:0, one launch (start us, length us, event | category | flops | bytes accessed | tf_op | source)
XLA Modules:
  0.0 89.7 jit_solution(3625344331916921360)
XLA Ops:
  7.2 1.0 %bitcast_multiply_fusion = bf16[768,256]{1,0:T(8,128)(2,1)S(1)} fusion(bf16[1,768,256]{2,1,0:T(8,128)(2,1)} %param.10, bf16[256]{0:T(256)(128)(2,1)S(1)} %compare_convert_fusion), kind=kLoop, calls=%fused_computation.33 | loop fusion | flops 196608 | bytes 786944 | tf_op jit(solution)/shard_map/mul | solution.py:34
  8.3 3.1 %collective-permute-start = (bf16[384,256]{1,0:T(8,128)(2,1)S(1)}, bf16[384,256]{1,0:T(8,128)(2,1)S(1)}, u32[]{:S(2)}, u32[]{:S(2)}) collective-permute-start(bf16[384,256]{1,0:T(8,128)(2,1)S(1)} %get-tuple-element.14), channel_id=1, source_target_pairs={{0,2},{2,4},{4,6},{6,0},{1,3},{3,5},{5,7},{7,1},{8,10},{10,12},{12... | collective-permute-start | bytes 589832 | tf_op jit(solution)/shard_map/ppermute | solution.py:15
  11.4 2.1 %collective-permute-start.1 = (bf16[384,256]{1,0:T(8,128)(2,1)S(1)}, bf16[384,256]{1,0:T(8,128)(2,1)S(1)}, u32[]{:S(2)}, u32[]{:S(2)}) collective-permute-start(bf16[384,256]{1,0:T(8,128)(2,1)S(1)} %get-tuple-element.15), channel_id=1, source_target_pairs={{2,0},{4,2},{6,4},{0,6},{3,1},{5,3},{7,5},{1,7},{10,8},{12,10},{14... | collective-permute-start | bytes 589832 | tf_op jit(solution)/shard_map/ppermute | solution.py:18
  13.5 0.3 slice_reduce_fusion
  13.7 0.6 compare_and_fusion.5
  14.3 0.6 compare_and_fusion.3
  14.9 0.6 compare_and_fusion
  15.5 0.6 pad_clamp_fusion
  17.4 0.6 compare_and_fusion.1
  18.0 1.2 %collective-permute-done = bf16[384,256]{1,0:T(8,128)(2,1)S(1)} collective-permute-done((bf16[384,256]{1,0:T(8,128)(2,1)S(1)}, bf16[384,256]{1,0:T(8,128)(2,1)S(1)}, u32[]{:S(2)}, u32[]{:S(2)}) %collective-permute-start) | collective-permute-done | bytes 196640 | tf_op jit(solution)/shard_map/ppermute | solution.py:15
  19.2 2.8 %collective-permute-done.1 = bf16[384,256]{1,0:T(8,128)(2,1)S(1)} collective-permute-done((bf16[384,256]{1,0:T(8,128)(2,1)S(1)}, bf16[384,256]{1,0:T(8,128)(2,1)S(1)}, u32[]{:S(2)}, u32[]{:S(2)}) %collective-permute-start.1) | collective-permute-done | bytes 196640 | tf_op jit(solution)/shard_map/ppermute | solution.py:18
  21.9 0.1 pad_maximum_fusion
  22.0 1.3 %gather_fusion = bf16[6,128,256]{2,1,0:T(8,128)(2,1)} fusion(bf16[12,128,256]{2,1,0:T(8,128)(2,1)S(1)} %bitcast.82, s32[1024]{0:T(1024)S(1)} %pad_clamp_fusion.5), kind=kCustom, calls=%fused_computation.clone | custom fusion | bytes 786456 | tf_op jit(solution)/shard_map/jit(_take)/gather | solution.py:43
  23.3 1.3 %gather_fusion.1 = bf16[6,128,256]{2,1,0:T(8,128)(2,1)} fusion(bf16[12,128,256]{2,1,0:T(8,128)(2,1)S(1)} %bitcast.83, s32[1024]{0:T(1024)S(1)} %pad_clamp_fusion.4), kind=kCustom, calls=%fused_computation.1.clone | custom fusion | bytes 786456 | tf_op jit(solution)/shard_map/jit(_take)/gather | solution.py:43
  24.7 0.6 gather_fusion.2
  25.3 0.0 copy-start
  25.3 0.6 gather_fusion.3
  25.9 0.6 gather_fusion.4
  26.4 0.7 gather_fusion.5
  27.2 1.4 %fusion.18 = f32[6,256,128]{1,2,0:T(8,128)S(1)} fusion(bf16[6,128,256]{2,1,0:T(8,128)(2,1)} %gather_fusion, pred[6]{0:T(512)(128)(4,1)} %get-tuple-element.22, bf16[6,6,128,128]{3,2,1,0:T(8,128)(2,1)S(1)} %copy-done), kind=kOutput, calls=%fused_computation.46 | convolution fusion | flops 50528256 | bytes 1376262 | tf_op jit(solution)/shard_map/rij,rjn->rin/dot_general | solution.py:44
  28.6 0.0 copy-done.5
  28.6 0.0 copy-done.18
  28.6 0.0 copy-start.10
  28.6 0.3 convolution_add_fusion.9
  28.9 0.3 copy-done.10
  29.2 0.3 convolution_add_fusion.8
  29.6 0.3 convolution_add_fusion.7
  30.0 0.2 copy-done.12
  30.2 0.3 convolution_add_fusion.6
  30.5 0.1 copy-done.20
  30.6 0.3 convolution_add_fusion.5
  31.0 0.6 copy-done.1
  31.6 0.1 fusion.2
  31.8 1.2 %collective-permute-start.2 = (bf16[384,256]{1,0:T(8,128)(2,1)S(1)}, bf16[384,256]{1,0:T(8,128)(2,1)S(1)}, u32[]{:S(2)}, u32[]{:S(2)}) collective-permute-start(bf16[384,256]{1,0:T(8,128)(2,1)S(1)} %get-tuple-element.12), channel_id=1, source_target_pairs={{0,2},{2,4},{4,6},{6,0},{1,3},{3,5},{5,7},{7,1},{8,10},{10,12},{12... | collective-permute-start | bytes 589832 | tf_op jit(solution)/shard_map/ppermute | solution.py:15
  33.0 2.7 %collective-permute-start.3 = (bf16[384,256]{1,0:T(8,128)(2,1)S(1)}, bf16[384,256]{1,0:T(8,128)(2,1)S(1)}, u32[]{:S(2)}, u32[]{:S(2)}) collective-permute-start(bf16[384,256]{1,0:T(8,128)(2,1)S(1)} %get-tuple-element.13), channel_id=1, source_target_pairs={{2,0},{4,2},{6,4},{0,6},{3,1},{5,3},{7,5},{1,7},{10,8},{12,10},{14... | collective-permute-start | bytes 589832 | tf_op jit(solution)/shard_map/ppermute | solution.py:18
  35.7 5.8 %collective-permute-done.2 = bf16[384,256]{1,0:T(8,128)(2,1)S(1)} collective-permute-done((bf16[384,256]{1,0:T(8,128)(2,1)S(1)}, bf16[384,256]{1,0:T(8,128)(2,1)S(1)}, u32[]{:S(2)}, u32[]{:S(2)}) %collective-permute-start.2) | collective-permute-done | bytes 196640 | tf_op jit(solution)/shard_map/ppermute | solution.py:15
  41.5 2.2 %collective-permute-done.3 = bf16[384,256]{1,0:T(8,128)(2,1)S(1)} collective-permute-done((bf16[384,256]{1,0:T(8,128)(2,1)S(1)}, bf16[384,256]{1,0:T(8,128)(2,1)S(1)}, u32[]{:S(2)}, u32[]{:S(2)}) %collective-permute-start.3) | collective-permute-done | bytes 196640 | tf_op jit(solution)/shard_map/ppermute | solution.py:18
  43.7 0.1 pad_maximum_fusion.1
  43.8 1.3 %gather_fusion.6 = bf16[6,128,256]{2,1,0:T(8,128)(2,1)} fusion(bf16[12,128,256]{2,1,0:T(8,128)(2,1)S(1)} %bitcast.76, s32[1024]{0:T(1024)S(1)} %pad_clamp_fusion.5), kind=kCustom, calls=%fused_computation.6.clone | custom fusion | bytes 786456 | tf_op jit(solution)/shard_map/jit(_take)/gather | solution.py:43
  45.1 1.3 %gather_fusion.7 = bf16[6,128,256]{2,1,0:T(8,128)(2,1)} fusion(bf16[12,128,256]{2,1,0:T(8,128)(2,1)S(1)} %bitcast.77, s32[1024]{0:T(1024)S(1)} %pad_clamp_fusion.4), kind=kCustom, calls=%fused_computation.7.clone | custom fusion | bytes 786456 | tf_op jit(solution)/shard_map/jit(_take)/gather | solution.py:43
  46.5 1.3 %gather_fusion.8 = bf16[6,128,256]{2,1,0:T(8,128)(2,1)} fusion(bf16[12,128,256]{2,1,0:T(8,128)(2,1)S(1)} %bitcast.78, s32[1024]{0:T(1024)S(1)} %pad_clamp_fusion.3), kind=kCustom, calls=%fused_computation.8.clone | custom fusion | bytes 786456 | tf_op jit(solution)/shard_map/jit(_take)/gather | solution.py:43
  47.8 1.3 %gather_fusion.9 = bf16[6,128,256]{2,1,0:T(8,128)(2,1)} fusion(bf16[12,128,256]{2,1,0:T(8,128)(2,1)S(1)} %bitcast.79, s32[1024]{0:T(1024)S(1)} %pad_clamp_fusion.2), kind=kCustom, calls=%fused_computation.9.clone | custom fusion | bytes 786456 | tf_op jit(solution)/shard_map/jit(_take)/gather | solution.py:43
  49.1 0.7 gather_fusion.10
  49.9 0.7 gather_fusion.11
  50.6 1.4 %fusion.11 = f32[6,256,128]{1,2,0:T(8,128)S(1)} fusion(bf16[6,128,256]{2,1,0:T(8,128)(2,1)} %gather_fusion.6, pred[6]{0:T(512)(128)(4,1)S(1)} %copy-done.7, bf16[6,6,128,128]{3,2,1,0:T(8,128)(2,1)S(1)} %copy-done), kind=kOutput, calls=%fused_computation.39 | convolution fusion | flops 50528256 | bytes 1376768 | tf_op jit(solution)/shard_map/rij,rjn->rin/dot_general | solution.py:44
  52.0 0.0 copy-done.19
  52.0 0.0 copy-done.4
  52.0 0.0 copy-start.3
  52.0 0.3 convolution_add_fusion.4
  52.4 0.6 copy-done.3
  53.0 0.3 convolution_add_fusion.3
  53.3 0.6 copy-done.2
  54.0 0.3 convolution_add_fusion.2
  54.3 0.3 copy-done.13
  54.6 0.3 convolution_add_fusion.1
  54.9 0.3 copy-done.21
  55.3 0.3 convolution_add_fusion
  55.6 0.3 copy-done.16
  55.9 0.2 fusion.3
  56.2 2.4 %all_gather.3 = bf16[768,512]{1,0:T(8,128)(2,1)S(1)} all-gather(bf16[768,256]{1,0:T(8,128)(2,1)S(1)} %fusion.3), channel_id=1, replica_groups=mesh['groups'=2,'cuts'=2,'row'=4,'sub'=2] {'sub'}, dimensions={1}, use_global_device_ids=true | all-gather | bytes 1179648 | tf_op jit(solution)/shard_map/all_gather | solution.py:59
  58.5 1.2 %fusion.82 = f32[256,512]{1,0:T(8,128)} fusion(bf16[768,256]{1,0:T(8,128)(2,1)S(1)} %fusion.3, bf16[768,512]{1,0:T(8,128)(2,1)S(1)} %all_gather.3), kind=kOutput, calls=%fused_computation.138 | convolution fusion | flops 201326592 | bytes 1703936 | tf_op jit(solution)/shard_map/rn,rm->nm/dot_general | solution.py:60
  59.7 0.0 reduce-scatter.2.cloned.1.call-update
  59.7 21.5 %reduce-scatter.2.cloned.1.call-done = f32[64,512]{1,0:T(8,128)} async-done(((f32[256,512]{1,0:T(8,128)}), f32[64,512]{1,0:T(8,128)}) %reduce-scatter.2.cloned.1.call-update) | async-done | bytes 131088 | tf_op jit(solution)/shard_map/reduce_scatter | solution.py:61
  81.3 1.6 %multiply_bitcast_fusion = f32[1,1,64,512]{3,2,1,0:T(8,128)} fusion(f32[64,512]{1,0:T(8,128)} %reduce-scatter.2.cloned.1.call-done), kind=kLoop, calls=%fused_computation.96 | loop fusion | flops 32768 | bytes 262144 | tf_op jit(solution)/shard_map/reshape | solution.py:63
  (41 shorter events, 0.2 us)
Async XLA Ops:
  6.5 6.9 %copy-start.17 = (s32[6,6]{1,0:T(8,128)S(1)}, s32[6,6]{1,0:T(8,128)}, u32[]{:S(2)}) copy-start(s32[6,6]{1,0:T(8,128)} %param.9) | copy-start | bytes 436
  6.5 74.7 %reduce-scatter.2.cloned.1.call-start = ((), (), s32[]{:S(2)}) async-start(), calls=%async_computation.1 | async-start | bytes 655360 | tf_op jit(solution)/shard_map/reduce_scatter | solution.py:61
  7.2 4.2 %copy-start.14 = (bf16[256]{0:T(256)(128)(2,1)}, bf16[256]{0:T(256)(128)(2,1)S(1)}, u32[]{:S(2)}) copy-start(bf16[256]{0:T(256)(128)(2,1)S(1)} %compare_convert_fusion) | copy-start | bytes 1540
  8.3 10.9 %collective-permute-start = (bf16[384,256]{1,0:T(8,128)(2,1)S(1)}, bf16[384,256]{1,0:T(8,128)(2,1)S(1)}, u32[]{:S(2)}, u32[]{:S(2)}) collective-permute-start(bf16[384,256]{1,0:T(8,128)(2,1)S(1)} %get-tuple-element.14), channel_id=1, source_target_pairs={{0,2},{2,4},{4,6},{6,0},{1,3},{3,5},{5,7},{7,1},{8,10},{10,12},{12... | collective-permute-start | bytes 589832 | tf_op jit(solution)/shard_map/ppermute | solution.py:15
  11.4 10.6 %collective-permute-start.1 = (bf16[384,256]{1,0:T(8,128)(2,1)S(1)}, bf16[384,256]{1,0:T(8,128)(2,1)S(1)}, u32[]{:S(2)}, u32[]{:S(2)}) collective-permute-start(bf16[384,256]{1,0:T(8,128)(2,1)S(1)} %get-tuple-element.15), channel_id=1, source_target_pairs={{2,0},{4,2},{6,4},{0,6},{3,1},{5,3},{7,5},{1,7},{10,8},{12,10},{14... | collective-permute-start | bytes 589832 | tf_op jit(solution)/shard_map/ppermute | solution.py:18
  15.5 10.3 %copy-start.6 = (s32[1024]{0:T(1024)}, s32[1024]{0:T(1024)S(1)}, u32[]{:S(2)}) copy-start(s32[1024]{0:T(1024)S(1)} %pad_clamp_fusion.1) | copy-start | bytes 12292
  25.3 1.9 %copy-start = (bf16[6,6,128,128]{3,2,1,0:T(8,128)(2,1)S(1)}, bf16[6,6,128,128]{3,2,1,0:T(8,128)(2,1)}, u32[]{:S(2)}) copy-start(bf16[6,6,128,128]{3,2,1,0:T(8,128)(2,1)} %param.8) | copy-start | bytes 3538948
  27.1 1.4 %copy-start.5 = (bf16[6,128,256]{2,1,0:T(8,128)(2,1)S(1)}, bf16[6,128,256]{2,1,0:T(8,128)(2,1)}, u32[]{:S(2)}) copy-start(bf16[6,128,256]{2,1,0:T(8,128)(2,1)} %gather_fusion.1) | copy-start | bytes 1179652
  27.1 1.4 %copy-start.18 = (pred[6]{0:T(512)(128)(4,1)S(1)}, pred[6]{0:T(512)(128)(4,1)}, u32[]{:S(2)}) copy-start(pred[6]{0:T(512)(128)(4,1)} %compare_and_fusion.5) | copy-start | bytes 22
  28.6 0.7 copy-start.10
  28.9 0.7 copy-start.8
  29.6 0.6 copy-start.12
  29.9 0.7 copy-start.20
  30.6 1.0 %copy-start.1 = (bf16[1,768,256]{2,1,0:T(8,128)(2,1)S(1)}, bf16[1,768,256]{2,1,0:T(8,128)(2,1)}, u32[]{:S(2)}) copy-start(bf16[1,768,256]{2,1,0:T(8,128)(2,1)} %param.10) | copy-start | bytes 1179652
  30.6 1.0 %copy-start.15 = (bf16[256]{0:T(256)(128)(2,1)S(1)}, bf16[256]{0:T(256)(128)(2,1)}, u32[]{:S(2)}) copy-start(bf16[256]{0:T(256)(128)(2,1)} %copy-done.14) | copy-start | bytes 1540
  31.8 9.7 %collective-permute-start.2 = (bf16[384,256]{1,0:T(8,128)(2,1)S(1)}, bf16[384,256]{1,0:T(8,128)(2,1)S(1)}, u32[]{:S(2)}, u32[]{:S(2)}) collective-permute-start(bf16[384,256]{1,0:T(8,128)(2,1)S(1)} %get-tuple-element.12), channel_id=1, source_target_pairs={{0,2},{2,4},{4,6},{6,0},{1,3},{3,5},{5,7},{7,1},{8,10},{10,12},{12... | collective-permute-start | bytes 589832 | tf_op jit(solution)/shard_map/ppermute | solution.py:15
  33.0 10.8 %collective-permute-start.3 = (bf16[384,256]{1,0:T(8,128)(2,1)S(1)}, bf16[384,256]{1,0:T(8,128)(2,1)S(1)}, u32[]{:S(2)}, u32[]{:S(2)}) collective-permute-start(bf16[384,256]{1,0:T(8,128)(2,1)S(1)} %get-tuple-element.13), channel_id=1, source_target_pairs={{2,0},{4,2},{6,4},{0,6},{3,1},{5,3},{7,5},{1,7},{10,8},{12,10},{14... | collective-permute-start | bytes 589832 | tf_op jit(solution)/shard_map/ppermute | solution.py:18
  47.8 2.8 %copy-start.7 = (pred[6]{0:T(512)(128)(4,1)S(1)}, pred[6]{0:T(512)(128)(4,1)}, u32[]{:S(2)}) copy-start(pred[6]{0:T(512)(128)(4,1)} %get-tuple-element.22) | copy-start | bytes 22
  49.8 2.1 %copy-start.19 = (pred[6]{0:T(512)(128)(4,1)S(1)}, pred[6]{0:T(512)(128)(4,1)}, u32[]{:S(2)}) copy-start(pred[6]{0:T(512)(128)(4,1)} %compare_and_fusion.5) | copy-start | bytes 22
  50.6 1.4 %copy-start.4 = (bf16[6,128,256]{2,1,0:T(8,128)(2,1)S(1)}, bf16[6,128,256]{2,1,0:T(8,128)(2,1)}, u32[]{:S(2)}) copy-start(bf16[6,128,256]{2,1,0:T(8,128)(2,1)} %gather_fusion.7) | copy-start | bytes 1179652
  52.0 1.0 %copy-start.3 = (bf16[6,128,256]{2,1,0:T(8,128)(2,1)S(1)}, bf16[6,128,256]{2,1,0:T(8,128)(2,1)}, u32[]{:S(2)}) copy-start(bf16[6,128,256]{2,1,0:T(8,128)(2,1)} %gather_fusion.8) | copy-start | bytes 1179652
  52.0 1.0 %copy-start.11 = (pred[6]{0:T(512)(128)(4,1)S(1)}, pred[6]{0:T(512)(128)(4,1)}, u32[]{:S(2)}) copy-start(pred[6]{0:T(512)(128)(4,1)} %get-tuple-element.25) | copy-start | bytes 22
  53.0 1.0 %copy-start.2 = (bf16[6,128,256]{2,1,0:T(8,128)(2,1)S(1)}, bf16[6,128,256]{2,1,0:T(8,128)(2,1)}, u32[]{:S(2)}) copy-start(bf16[6,128,256]{2,1,0:T(8,128)(2,1)} %gather_fusion.9) | copy-start | bytes 1179652
  53.0 1.0 %copy-start.9 = (pred[6]{0:T(512)(128)(4,1)S(1)}, pred[6]{0:T(512)(128)(4,1)}, u32[]{:S(2)}) copy-start(pred[6]{0:T(512)(128)(4,1)} %get-tuple-element.24) | copy-start | bytes 22
  54.0 0.6 copy-start.13
  54.6 0.7 copy-start.21
  55.3 0.7 copy-start.16
Sparse Core Ops, SparseCore 0:
  59.9 21.3 reduce-scatter.1
where the time goes:
time: 90.1 us; the launch traced here: 89.7 us
  waiting for transfers between devices  33.5 us (37%)
  between operations  15.8 us (18%)
  local copies, waits for them, and re-layouts  15.7 us (17%)
  starting transfers between devices  9.05 us (10%)
  matrix products  7.31 us (8%)
  other arithmetic  6 us (7%)
  blocking collectives  2.37 us (3%)
    reduce_scatter x1, waiting for transfers between devices, body(): gram = lax.psum_scatter(term, 'row', scatter_dimension=0, tiled=True)  21.5 us
    gather x12, local copies, waits for them, and re-layouts, apply_hop(): picked = jnp.take(blocks, local_index[:, k], axis=0)  11.8 us
    ppermute x2, waiting for transfers between devices, with_halo(): lax.ppermute(lax.slice_in_dim(block, block.shape[dim] - width, None, axis...  6.99 us
    dot_general x12, matrix products, apply_hop(): jnp.einsum('rij,rjn->rin', hop[:, k], picked, preferred_element_type=jnp....  6.12 us
    ppermute x2, waiting for transfers between devices, with_halo(): lax.ppermute(lax.slice_in_dim(block, 0, width, axis=dim), axis, backward)  5.01 us
    ppermute x2, starting transfers between devices, with_halo(): lax.ppermute(lax.slice_in_dim(block, 0, width, axis=dim), axis, backward)  4.79 us
    ppermute x2, starting transfers between devices, with_halo(): lax.ppermute(lax.slice_in_dim(block, block.shape[dim] - width, None, axis...  4.26 us
    unnamed x44, local copies, waits for them, and re-layouts  3.52 us
  transfers between devices with their start and end apart: 5, of which 5 were waited for; matrix products, arithmetic and copies ran while one was open for 4% of the time, Pallas kernels for 0%

commit v1 on v0

v1 whole, which is shorter than its diff:
```python
import functools

import jax
import jax.numpy as jnp
from jax import lax
from jax.experimental import pallas as pl
from jax.experimental.pallas import tpu as pltpu
from jax.sharding import PartitionSpec as P

W = 3
MESH = pl.DeviceIdType.MESH
PEAK = 32767.0
FLOOR = 1e-33


def dot(a, b):
    return jnp.dot(a, b, preferred_element_type=jnp.float32)


def kernel(
    n, rows, bs, half, nnz,
    pattern, counts, center, width, hop_hbm, vec_hbm, out,
    hop, band, ext0, ext1, acc, fil, qsend, qrecv, ssend, srecv, own,
    load_sem, h1_send, h1_recv, h2_send, h2_recv, f_send, f_recv, g_send, g_recv, c_send, c_recv,
):
    me = lax.axis_index("row")
    sub = lax.axis_index("sub")
    other = 1 - sub
    right, left = lax.rem(me + 1, n), lax.rem(me + n - 1, n)
    total_blocks = n * rows
    share = half // n
    top = W + rows

    def at(block):
        return pl.ds(block * bs, bs)

    load_v = pltpu.make_async_copy(
        vec_hbm.at[0], ext0.at[pl.ds(W * bs, rows * bs)], load_sem.at[0]
    )
    load_h = pltpu.make_async_copy(hop_hbm, hop, load_sem.at[1])
    load_v.start()
    load_h.start()

    barrier = pltpu.get_barrier_semaphore()
    for d in range(1, n):
        pl.semaphore_signal(
            barrier, inc=1, device_id={"row": lax.rem(me + d, n)}, device_id_type=MESH
        )
    pl.semaphore_signal(barrier, inc=1, device_id={"sub": other}, device_id_type=MESH)
    pl.semaphore_wait(barrier, n)

    def to_row(src, dst, send, recv, target):
        return pltpu.make_async_remote_copy(
            src_ref=src, dst_ref=dst, send_sem=send, recv_sem=recv,
            device_id={"row": target}, device_id_type=MESH,
        )

    first = []
    for j in range(W):
        up = to_row(
            vec_hbm.at[0, at(rows - 1 - j)], ext0.at[at(W - 1 - j)],
            h1_send.at[j], h1_recv.at[j], right,
        )
        down = to_row(
            vec_hbm.at[0, at(j)], ext0.at[at(top + j)],
            h1_send.at[W + j], h1_recv.at[W + j], left,
        )
        up.start()
        down.start()
        first.append((up, down))

    live = (
        lax.broadcasted_iota(jnp.int32, (1, half), 1) + sub * half < counts[0]
    )
    shift = center[0]
    inverse = 1.0 / jnp.full((1, half), width[0], jnp.float32)

    def mask(block):
        part = ext0[at(block), :]
        ext0[at(block), :] = jnp.where(live, part, jnp.zeros_like(part))

    load_h.wait()
    for i in range(rows):
        for o in range(2 * W + 1):
            want = lax.rem(me * rows + i + o - W + total_blocks, total_blocks)
            where = jnp.int32(0)
            found = jnp.int32(0)
            for k in range(nnz):
                hit = pattern[i, k] == want
                where = jnp.where(hit, k, where)
                found = jnp.where(hit, 1, found)
            block = hop[i, where]
            present = jnp.full((bs, bs), found, jnp.int32) > 0
            band[i, :, o * bs : (o + 1) * bs] = jnp.where(
                present, block.astype(jnp.float32), 0.0
            ).astype(jnp.bfloat16)

    load_v.wait()
    for i in range(rows):
        mask(W + i)

    def piece(i, low, high, ext):
        return dot(
            band[i, :, (low - i) * bs : (high - i) * bs], ext[low * bs : high * bs, :]
        )

    def local(i, ext):
        return piece(i, max(i, W), min(i + 2 * W + 1, top), ext)

    for i in range(rows):
        acc[at(i), :] = local(i, ext0)

    second = []

    def finish_one(i):
        start = ext0[at(W + i), :].astype(jnp.float32)
        ext1[at(W + i), :] = ((acc[at(i), :] - shift * start) * inverse).astype(
            jnp.bfloat16
        )

    for j in range(W):
        up, down = first[j]
        low, high = W - 1 - j, rows - W + j
        up.wait_recv()
        mask(low)
        acc[at(low), :] += piece(low, low, W, ext0)
        finish_one(low)
        go_left = to_row(
            ext1.at[at(W + low)], ext1.at[at(top + low)],
            h2_send.at[j], h2_recv.at[j], left,
        )
        go_left.start()
        down.wait_recv()
        mask(top + j)
        acc[at(high), :] += piece(high, top, top + j + 1, ext0)
        finish_one(high)
        go_right = to_row(
            ext1.at[at(W + high)], ext1.at[at(j)],
            h2_send.at[W + j], h2_recv.at[W + j], right,
        )
        go_right.start()
        second.append((go_left, go_right))

    for i in range(rows):
        acc[at(i), :] = local(i, ext1)

    for j in range(W):
        go_left, go_right = second[j]
        go_right.wait_recv()
        for i in range(j + 1):
            acc[at(i), :] += piece(i, j, j + 1, ext1)
        go_left.wait_recv()
        block = top + W - 1 - j
        for i in range(block - 2 * W, rows):
            acc[at(i), :] += piece(i, block, block + 1, ext1)

    sides = []
    for i in range(rows):
        start = ext0[at(W + i), :].astype(jnp.float32)
        one = ext1[at(W + i), :].astype(jnp.float32)
        fil[0, at(i), :] = (
            2.0 * (acc[at(i), :] - shift * one) * inverse - start
        ).astype(jnp.bfloat16)
        side = pltpu.make_async_remote_copy(
            src_ref=fil.at[0, at(i)], dst_ref=fil.at[1, at(i)],
            send_sem=f_send.at[i], recv_sem=f_recv.at[i],
            device_id={"sub": other}, device_id_type=MESH,
        )
        side.start()
        sides.append(side)

    mine = fil[0].T
    sends = []
    for p in range(2):
        if p:
            for side in sides:
                side.wait_recv()
        term = dot(mine, fil[p])
        own[p] = term.reshape(n, share, half)
        for t in range(n):
            part = term[t * share : (t + 1) * share, :]
            peak = jnp.maximum(jnp.max(jnp.abs(part), axis=0, keepdims=True), FLOOR)
            qsend[p, t] = jnp.round(part * (PEAK / peak)).astype(jnp.int32).astype(qsend.dtype)
            ssend[p, t] = peak * (1.0 / PEAK)
        for d in range(1, n):
            target = lax.rem(me + d, n)
            values = to_row(
                qsend.at[p, target], qrecv.at[p, d - 1],
                g_send.at[p, d - 1], g_recv.at[p, d - 1], target,
            )
            scales = to_row(
                ssend.at[p, target], srecv.at[p, d - 1],
                c_send.at[p, d - 1], c_recv.at[p, d - 1], target,
            )
            scales.start()
            values.start()
            sends.append((p, d, values, scales))

    scale = 1.0 / (total_blocks * bs)
    for p in range(2):
        total = own[p, me]
        for q, d, values, scales in sends:
            if q == p:
                scales.wait_recv()
                values.wait_recv()
                total = total + qrecv[p, d - 1].astype(jnp.int32).astype(
                    jnp.float32
                ) * srecv[p, d - 1]
        column = sub if p == 0 else other
        out[:, pl.ds(pl.multiple_of(column * half, half), half)] = total * scale

    for pair in first + second:
        for copy in pair:
            copy.wait_send()
    for side in sides:
        side.wait_send()
    for _, _, values, scales in sends:
        values.wait_send()
        scales.wait_send()


def body(hop, pattern, vectors, counts, center, halfwidth):
    rows, nnz, bs, _ = hop.shape
    half = vectors.shape[2]
    n = lax.axis_size("row")
    share = half // n
    code = jnp.int16 if share % 16 == 0 else jnp.int32
    dma = pltpu.SemaphoreType.DMA
    smem = pl.BlockSpec(memory_space=pltpu.SMEM)
    hbm = pl.BlockSpec(memory_space=pl.ANY)
    flops = 2 * rows * bs * half * (2 * (2 * W + 1) * bs + 2 * half)
    margin = pl.pallas_call(
        functools.partial(kernel, n, rows, bs, half, nnz),
        out_shape=jax.ShapeDtypeStruct((share, 2 * half), jnp.float32),
        in_specs=[smem, smem, smem, smem, hbm, hbm],
        out_specs=pl.BlockSpec(memory_space=pltpu.VMEM),
        scratch_shapes=[
            pltpu.VMEM(hop.shape, jnp.bfloat16),
            pltpu.VMEM((rows, bs, (2 * W + 1) * bs), jnp.bfloat16),
            pltpu.VMEM(((rows + 2 * W) * bs, half), jnp.bfloat16),
            pltpu.VMEM(((rows + 2 * W) * bs, half), jnp.bfloat16),
            pltpu.VMEM((rows * bs, half), jnp.float32),
            pltpu.VMEM((2, rows * bs, half), jnp.bfloat16),
            pltpu.VMEM((2, n, share, half), code),
            pltpu.VMEM((2, n - 1, share, half), code),
            pltpu.VMEM((2, n, 1, half), jnp.float32),
            pltpu.VMEM((2, n - 1, 1, half), jnp.float32),
            pltpu.VMEM((2, n, share, half), jnp.float32),
            dma((2,)),
            dma((2 * W,)), dma((2 * W,)), dma((2 * W,)), dma((2 * W,)),
            dma((rows,)), dma((rows,)),
            dma((2, n - 1)), dma((2, n - 1)), dma((2, n - 1)), dma((2, n - 1)),
        ],
        compiler_params=pltpu.CompilerParams(
            collective_id=0, has_side_effects=True, vmem_limit_bytes=40 * 2**20
        ),
        cost_estimate=pl.CostEstimate(
            flops=flops, bytes_accessed=2 * (hop.size + vectors.size), transcendentals=0
        ),
    )(pattern, counts, center, halfwidth, hop, vectors)
    return margin.reshape(1, 1, share, 2 * half)


def solution(mesh):
    in_specs = (
        P(("groups", "row"), None, None, None),
        P(("groups", "row"), None),
        P("cuts", ("groups", "row"), "sub"),
        P(("groups", "cuts")),
        P(("groups", "cuts")),
        P(("groups", "cuts")),
    )
    out_specs = P(("groups", "cuts"), "sub", "row", None)
    return jax.shard_map(body, mesh=mesh, in_specs=in_specs, out_specs=out_specs, check_vma=False)
```

time: 90.1 us -> 37.4 us (0.42)
  waiting for transfers between devices: 33.5 us -> 0 us
  Pallas kernels: 0 us -> 31.5 us
  between operations: 15.8 us -> 1.96 us
  local copies, waits for them, and re-layouts: 15.7 us -> 3.6 us
  starting transfers between devices: 9.05 us -> 0 us
  matrix products: 7.31 us -> 0 us
  other arithmetic: 6 us -> 0 us
  blocking collectives: 2.37 us -> 0 us
    pallas_call x0 -> x1, Pallas kernels: none -> 31.5 us  [body(): pl.pallas_call(functools.partial(kernel, n, rows, bs, half, nnz), out_sha...]
    reduce_scatter x1 -> x0, waiting for transfers between devices: 21.5 us -> none  [body(): gram = lax.psum_scatter(term, 'row', scatter_dimension=0, tiled=True)]
    ppermute x4 -> x0, waiting for transfers between devices: 12 us -> none  [the longest x2 6.99 us: with_halo(): lax.ppermute(lax.slice_in_dim(block, block.shape[dim] - width, None, axis...]
    gather x12 -> x0, local copies, waits for them, and re-layouts: 11.8 us -> none  [apply_hop(): picked = jnp.take(blocks, local_index[:, k], axis=0)]
    ppermute x4 -> x0, starting transfers between devices: 9.05 us -> none  [the longest x2 4.79 us: with_halo(): lax.ppermute(lax.slice_in_dim(block, 0, width, axis=dim), axis, backward)]
    dot_general x13 -> x0, matrix products: 7.31 us -> none  [the longest x12 6.12 us: apply_hop(): jnp.einsum('rij,rjn->rin', hop[:, k], picked, preferred_element_type=jnp....]
    all_gather x1 -> x0, blocking collectives: 2.37 us -> none  [body(): full_cols = lax.all_gather(filtered, 'sub', axis=1, tiled=True)]
    and x4 -> x0, other arithmetic: 2.27 us -> none  [apply_hop(): picked = jnp.take(blocks, local_index[:, k], axis=0)]
  transfers between devices with their start and end apart: 5 -> 0, of which waited for: 5 -> 0; matrix products, arithmetic and copies ran while one was open for 4% -> 0% of each run, Pallas kernels for 0% -> 0%
where the time goes in v1:
time: 37.4 us; the launch traced here: 37.1 us
  Pallas kernels  31.5 us (84%)
  local copies, waits for them, and re-layouts  3.6 us (10%)
  between operations  1.96 us (5%)
    pallas_call x1, Pallas kernels, body(): pl.pallas_call(functools.partial(kernel, n, rows, bs, half, nnz), out_sha...  31.5 us
    unnamed x7, local copies, waits for them, and re-layouts  3.6 us

profile of v1, /device:TPU:0, one launch (start us, length us, event | category | flops | bytes accessed | tf_op | source)
XLA Modules:
  0.0 37.1 jit_solution(14236558892463868140)
XLA Ops:
  1.9 0.0 copy-start
  2.0 1.3 %copy-done = bf16[6,6,128,128]{3,2,1,0:T(8,128)(2,1)S(1)} copy-done((bf16[6,6,128,128]{3,2,1,0:T(8,128)(2,1)S(1)}, bf16[6,6,128,128]{3,2,1,0:T(8,128)(2,1)}, u32[]{:S(2)}) %copy-start) | copy-done | bytes 1179672
  3.2 0.0 copy-start.1
  3.2 1.0 %copy-done.1 = bf16[1,768,256]{2,1,0:T(8,128)(2,1)S(1)} copy-done((bf16[1,768,256]{2,1,0:T(8,128)(2,1)S(1)}, bf16[1,768,256]{2,1,0:T(8,128)(2,1)}, u32[]{:S(2)}) %copy-start.1) | copy-done | bytes 393240
  4.2 0.0 copy-start.2
  4.2 0.7 %copy-done.2 = s32[6,6]{1,0:T(8,128)S(1)} copy-done((s32[6,6]{1,0:T(8,128)S(1)}, s32[6,6]{1,0:T(8,128)}, u32[]{:S(2)}) %copy-start.2) | copy-done | bytes 168
  4.9 31.5 %shard_map.64 = f32[64,512]{1,0:T(8,128)S(1)} custom-call(s32[6,6]{1,0:T(8,128)S(1)} %copy-done.2, s32[1]{0:T(128)S(6)} %copy.8.counts, f32[1]{0:T(128)S(6)} %copy.9.center, f32[1]{0:T(128)S(6)} %copy.10.width, bf16[6,6,128,128]{3,2,1,0:T(8,128)(2,1)S(1)} %copy-done, bf16[1,768,256]{2,1,0:T(8,128)(2,1)S(1)} %copy-done.1), custom_call_target="tpu_custom_call" | custom-call | flops 905969664 | bytes 1572864 | tf_op jit(solution)/shard_map/pallas_call | solution.py:232
  36.5 0.7 %copy.11 = f32[1,1,64,512]{3,2,1,0:T(8,128)} copy(f32[1,1,64,512]{3,2,1,0:T(8,128)S(1)} %bitcast.1) | data formatting | bytes 262144
Async XLA Ops:
  1.9 1.3 %copy-start = (bf16[6,6,128,128]{3,2,1,0:T(8,128)(2,1)S(1)}, bf16[6,6,128,128]{3,2,1,0:T(8,128)(2,1)}, u32[]{:S(2)}) copy-start(bf16[6,6,128,128]{3,2,1,0:T(8,128)(2,1)} %hop_hbm.1) | copy-start | bytes 3538948
  3.2 1.0 %copy-start.1 = (bf16[1,768,256]{2,1,0:T(8,128)(2,1)S(1)}, bf16[1,768,256]{2,1,0:T(8,128)(2,1)}, u32[]{:S(2)}) copy-start(bf16[1,768,256]{2,1,0:T(8,128)(2,1)} %vec_hbm.1) | copy-start | bytes 1179652
  4.2 0.7 %copy-start.2 = (s32[6,6]{1,0:T(8,128)S(1)}, s32[6,6]{1,0:T(8,128)}, u32[]{:S(2)}) copy-start(s32[6,6]{1,0:T(8,128)} %pattern.1) | copy-start | bytes 436

commit v2 on v1

--- a/solution.py
+++ b/solution.py
@@ -19,7 +19,8 @@
 
 def kernel(
     n, rows, bs, half, nnz,
-    pattern, counts, center, width, hop_hbm, vec_hbm, out,
+    pattern_hbm, counts_hbm, center_hbm, width_hbm, hop_hbm, vec_hbm, out,
+    pattern, counts, center, width,
     hop, band, ext0, ext1, acc, fil, qsend, qrecv, ssend, srecv, own,
     load_sem, h1_send, h1_recv, h2_send, h2_recv, f_send, f_recv, g_send, g_recv, c_send, c_recv,
 ):
@@ -38,6 +39,17 @@
         vec_hbm.at[0], ext0.at[pl.ds(W * bs, rows * bs)], load_sem.at[0]
     )
     load_h = pltpu.make_async_copy(hop_hbm, hop, load_sem.at[1])
+    small = [
+        pltpu.make_async_copy(source, here, load_sem.at[2 + i])
+        for i, (source, here) in enumerate(
+            (
+                (pattern_hbm, pattern), (counts_hbm, counts),
+                (center_hbm, center), (width_hbm, width),
+            )
+        )
+    ]
+    for copy in small:
+        copy.start()
     load_v.start()
     load_h.start()
 
@@ -69,6 +81,8 @@
         down.start()
         first.append((up, down))
 
+    for copy in small:
+        copy.wait()
     live = (
         lax.broadcasted_iota(jnp.int32, (1, half), 1) + sub * half < counts[0]
     )
@@ -226,15 +240,18 @@
     share = half // n
     code = jnp.int16 if share % 16 == 0 else jnp.int32
     dma = pltpu.SemaphoreType.DMA
-    smem = pl.BlockSpec(memory_space=pltpu.SMEM)
-    hbm = pl.BlockSpec(memory_space=pl.ANY)
+    hbm = pl.BlockSpec(memory_space=pltpu.HBM)
     flops = 2 * rows * bs * half * (2 * (2 * W + 1) * bs + 2 * half)
     margin = pl.pallas_call(
         functools.partial(kernel, n, rows, bs, half, nnz),
         out_shape=jax.ShapeDtypeStruct((share, 2 * half), jnp.float32),
-        in_specs=[smem, smem, smem, smem, hbm, hbm],
+        in_specs=[hbm] * 6,
         out_specs=pl.BlockSpec(memory_space=pltpu.VMEM),
         scratch_shapes=[
+            pltpu.SMEM(pattern.shape, jnp.int32),
+            pltpu.SMEM(counts.shape, jnp.int32),
+            pltpu.SMEM(center.shape, jnp.float32),
+            pltpu.SMEM(halfwidth.shape, jnp.float32),
             pltpu.VMEM(hop.shape, jnp.bfloat16),
             pltpu.VMEM((rows, bs, (2 * W + 1) * bs), jnp.bfloat16),
             pltpu.VMEM(((rows + 2 * W) * bs, half), jnp.bfloat16),
@@ -246,13 +263,13 @@
             pltpu.VMEM((2, n, 1, half), jnp.float32),
             pltpu.VMEM((2, n - 1, 1, half), jnp.float32),
             pltpu.VMEM((2, n, share, half), jnp.float32),
-            dma((2,)),
+            dma((6,)),
             dma((2 * W,)), dma((2 * W,)), dma((2 * W,)), dma((2 * W,)),
             dma((rows,)), dma((rows,)),
             dma((2, n - 1)), dma((2, n - 1)), dma((2, n - 1)), dma((2, n - 1)),
         ],
         compiler_params=pltpu.CompilerParams(
-            collective_id=0, has_side_effects=True, vmem_limit_bytes=40 * 2**20
+            collective_id=0, has_side_effects=True, vmem_limit_bytes=62 * 2**20
         ),
         cost_estimate=pl.CostEstimate(
             flops=flops, bytes_accessed=2 * (hop.size + vectors.size), transcendentals=0

time: 37.4 us -> 35.1 us (0.939)
  local copies, waits for them, and re-layouts: 3.6 us -> 1.57 us
    unnamed x7 -> x1, local copies, waits for them, and re-layouts: 3.6 us -> 1.57 us
where the time goes in v2:
time: 35.1 us; the launch traced here: 34.9 us
  Pallas kernels  31.4 us (89%)
  between operations  1.95 us (6%)
  local copies, waits for them, and re-layouts  1.57 us (4%)
    pallas_call x1, Pallas kernels, body(): pl.pallas_call(functools.partial(kernel, n, rows, bs, half, nnz), out_sha...  31.4 us
    unnamed x1, local copies, waits for them, and re-layouts  1.57 us

profile of v2, /device:TPU:0, one launch (start us, length us, event | category | flops | bytes accessed | tf_op | source)
XLA Modules:
  0.0 34.9 jit_solution(12084075323389885272)
XLA Ops:
  1.9 31.4 %shard_map.64 = f32[64,512]{1,0:T(8,128)} custom-call(s32[6,6]{1,0:T(8,128)} %pattern_hbm.1, s32[1]{0:T(128)S(6)} %copy.8.counts_hbm, f32[1]{0:T(128)S(6)} %copy.9.center_hbm, f32[1]{0:T(128)S(6)} %copy.10.width_hbm, bf16[6,6,128,128]{3,2,1,0:T(8,128)(2,1)} %hop_hbm.1, bf16[1,768,256]{2,1,0:T(8,128)(2,1)} %vec_hbm.1), custom_call_target="tpu_custom_call" | custom-call | flops 905969664 | bytes 1572864 | tf_op jit(solution)/shard_map/pallas_call | solution.py:245
  33.4 1.6 %copy.11 = f32[1,1,64,512]{3,2,1,0:T(8,128)} copy(f32[1,1,64,512]{3,2,1,0:T(8,128)} %bitcast.1) | data formatting | bytes 262144

commit v3 on v2

--- a/solution.py
+++ b/solution.py
@@ -242,6 +242,9 @@
     dma = pltpu.SemaphoreType.DMA
     hbm = pl.BlockSpec(memory_space=pltpu.HBM)
     flops = 2 * rows * bs * half * (2 * (2 * W + 1) * bs + 2 * half)
+    hop, pattern, vectors = (
+        pltpu.with_memory_space_constraint(x, pltpu.HBM) for x in (hop, pattern, vectors)
+    )
     margin = pl.pallas_call(
         functools.partial(kernel, n, rows, bs, half, nnz),
         out_shape=jax.ShapeDtypeStruct((share, 2 * half), jnp.float32),
@@ -269,7 +272,7 @@
             dma((2, n - 1)), dma((2, n - 1)), dma((2, n - 1)), dma((2, n - 1)),
         ],
         compiler_params=pltpu.CompilerParams(
-            collective_id=0, has_side_effects=True, vmem_limit_bytes=62 * 2**20
+            collective_id=0, has_side_effects=True, vmem_limit_bytes=40 * 2**20
         ),
         cost_estimate=pl.CostEstimate(
             flops=flops, bytes_accessed=2 * (hop.size + vectors.size), transcendentals=0

time: 35.1 us -> 33.6 us (0.957)
  local copies, waits for them, and re-layouts: 1.57 us -> 0.66 us
  Pallas kernels: 31.4 us -> 30.8 us
    unnamed x1, local copies, waits for them, and re-layouts: 1.57 us -> 0.66 us
    pallas_call x1, Pallas kernels: 31.4 us -> 30.8 us  [body(): pl.pallas_call(functools.partial(kernel, n, rows, bs, half, nnz), out_sha...]
where the time goes in v3:
time: 33.6 us; the launch traced here: 33.4 us
  Pallas kernels  30.8 us (92%)
  between operations  1.95 us (6%)
  local copies, waits for them, and re-layouts  0.66 us (2%)
    pallas_call x1, Pallas kernels, body(): pl.pallas_call(functools.partial(kernel, n, rows, bs, half, nnz), out_sha...  30.8 us

profile of v3, /device:TPU:0, one launch (start us, length us, event | category | flops | bytes accessed | tf_op | source)
XLA Modules:
  0.0 33.4 jit_solution(3901060241892069344)
XLA Ops:
  1.9 30.8 %shard_map.64 = f32[64,512]{1,0:T(8,128)S(1)} custom-call(s32[6,6]{1,0:T(8,128)} %pattern_hbm.1, s32[1]{0:T(128)S(6)} %copy.8.counts_hbm, f32[1]{0:T(128)S(6)} %copy.9.center_hbm, f32[1]{0:T(128)S(6)} %copy.10.width_hbm, bf16[6,6,128,128]{3,2,1,0:T(8,128)(2,1)} %hop_hbm.1, bf16[1,768,256]{2,1,0:T(8,128)(2,1)} %vec_hbm.1), custom_call_target="tpu_custom_call" | custom-call | flops 905969664 | bytes 1572864 | tf_op jit(solution)/shard_map/pallas_call | solution.py:248
  32.7 0.7 %copy.11 = f32[1,1,64,512]{3,2,1,0:T(8,128)} copy(f32[1,1,64,512]{3,2,1,0:T(8,128)S(1)} %bitcast.1) | data formatting | bytes 262144
